TPU v7x, 32 devices: a whole 2x2x4 slice. The times are simulated.
32 devices in a mesh: groups: 2 (over y), seq: 4 (over z), head: 2 (over x), batch: 2 (over core).
Axes of the slice: x: 2, y: 2, z: 4, core: 2. Of those that a mesh axis runs over, the one named last changes fastest.
Arguments:
- query_rows: bfloat16 [4, 4096, 1024], P(('groups', 'batch'), 'seq', 'head'), parts along dimension 0, may hold values from -32 to 32
- key_rows: bfloat16 [4, 4096, 1024], P(('groups', 'batch'), 'seq', 'head'), parts along dimension 0, may hold values from -32 to 32
- value_rows: bfloat16 [4, 4096, 1024], P(('groups', 'batch'), 'seq', 'head'), parts along dimension 0, may hold values from -6 to 6
- grad_output: bfloat16 [4, 4096, 1024], P(('groups', 'batch'), 'seq', 'head'), parts along dimension 0, may hold values from -6 to 6
Outputs:
- grad_queries: bfloat16 [4, 4096, 1024], P(('groups', 'batch'), 'seq', 'head'), parts along dimension 0
- grad_keys: bfloat16 [4, 4096, 1024], P(('groups', 'batch'), 'seq', 'head'), parts along dimension 0
- grad_values: bfloat16 [4, 4096, 1024], P(('groups', 'batch'), 'seq', 'head'), parts along dimension 0
There are 2 independent parts, one for each index of `groups`. A program takes and returns all parts, laid end to end along the dimension named above; each array names one. Nothing has to cross between parts.
All inputs are finite; a program needn't handle non-finite values. Where the computation divides by a largest or mean magnitude, that divisor is 1e-20 or more.
Results may differ from a plain program's by a relative error of at most 0.023.
The roundings to bfloat16 on the way count: a program that leaves them out, or rounds other values in their place, can miss the bound.
Values may be sent and summed in bfloat16 or wider, within the bound.
A program may use at most 128 MiB of HBM per device.

v0:
```python
import jax
import jax.numpy as jnp
from jax import lax
from jax.sharding import PartitionSpec as P

DH = 64
M = 256
ITERS = 4


def joined(x, axis, combine):
    everything = jax.tree.map(lambda part: lax.all_gather(part, axis), x)
    leading = jax.tree.map(lambda part: part[0], everything)

    def turn(k, so_far):
        return combine(so_far, jax.tree.map(lambda part: part[k], everything))

    return lax.fori_loop(1, lax.axis_size(axis), turn, leading)


def newton(matrix):
    size = matrix.shape[-1]
    identity = jnp.eye(size, dtype=matrix.dtype)
    col_norm = jnp.max(jnp.sum(jnp.abs(matrix), axis=-2), axis=-1)
    row_norm = jnp.max(jnp.sum(jnp.abs(matrix), axis=-1), axis=-1)
    approx = jnp.swapaxes(matrix, -1, -2) / (col_norm * row_norm)[..., None, None]
    for sweep in range(ITERS):
        product = jnp.matmul(matrix, approx, precision=lax.Precision.HIGHEST)
        inner = jnp.matmul(product, 7.0 * identity - product, precision=lax.Precision.HIGHEST)
        inner = jnp.matmul(product, 15.0 * identity - inner, precision=lax.Precision.HIGHEST)
        approx = 0.25 * jnp.matmul(approx, 13.0 * identity - inner, precision=lax.Precision.HIGHEST)
    return approx


def normalize(scores):
    shifted = jnp.exp(scores - jnp.max(scores, axis=-1, keepdims=True))
    return shifted / jnp.sum(shifted, axis=-1, keepdims=True)


def combine_stats(first, second):
    top = jnp.maximum(first[0], second[0])
    total = first[1] * jnp.exp(first[0] - top) + second[1] * jnp.exp(second[0] - top)
    return (top, total)


def per_device(query_rows, key_rows, value_rows, grad_output):
    high = lax.Precision.HIGHEST
    count, rows, width = query_rows.shape
    heads = width // DH
    spread = lax.axis_size("seq")
    land_dev = M // spread
    seg_len = rows // land_dev
    temper = DH ** (-0.5)

    def landmarks(data):
        summed = jnp.sum(data.reshape(count, land_dev, seg_len, width), axis=2, dtype=jnp.float32)
        return (summed / seg_len).astype(jnp.bfloat16)

    land_q, land_k = (
        lax.all_gather(landmarks(query_rows), "seq", axis=1, tiled=True),
        lax.all_gather(landmarks(key_rows), "seq", axis=1, tiled=True),
    )
    quer = query_rows.reshape(count, rows, heads, DH)
    keys_four = key_rows.reshape(count, rows, heads, DH)
    vals_four = value_rows.reshape(count, rows, heads, DH)
    grad_four = grad_output.reshape(count, rows, heads, DH)
    landq_four = land_q.reshape(count, M, heads, DH)
    landk_four = land_k.reshape(count, M, heads, DH)
    soft_f = normalize(
        temper * jnp.einsum("blhd,bmhd->bhlm", quer, landk_four, preferred_element_type=jnp.float32)
    )
    soft_a = normalize(
        temper
        * jnp.einsum("bmhd,bnhd->bhmn", landq_four, landk_four, preferred_element_type=jnp.float32)
    )
    inverse, pull = jax.vjp(newton, soft_a)
    scores_b = temper * jnp.einsum(
        "bmhd,blhd->bhml", landq_four, keys_four, preferred_element_type=jnp.float32
    )
    local_max = jnp.max(scores_b, axis=-1)
    local_sum = jnp.sum(jnp.exp(scores_b - local_max[..., None]), axis=-1)
    top, total = joined((local_max, local_sum), "seq", combine_stats)
    soft_b = jnp.exp(scores_b - top[..., None]) / total[..., None]
    weights_b = soft_b.astype(jnp.bfloat16)
    mix_part = jnp.einsum(
        "bhml,blhd->bmhd", weights_b, vals_four, preferred_element_type=jnp.float32
    ).reshape(count, M, width)
    weights_f = soft_f.astype(jnp.bfloat16)
    comb_part = jnp.einsum(
        "bhlm,blhd->bmhd", weights_f, grad_four, preferred_element_type=jnp.float32
    ).reshape(count, M, width)
    mixed = lax.psum(mix_part, "seq")
    grad_comb = lax.psum(comb_part, "seq")
    mixed_four = mixed.reshape(count, M, heads, DH)
    gcomb_four = grad_comb.reshape(count, M, heads, DH)
    combined = jnp.einsum("bhmn,bnhd->bmhd", inverse, mixed_four, precision=high).astype(
        jnp.bfloat16
    )
    grad_f = jnp.einsum("blhd,bmhd->bhlm", grad_four, combined, preferred_element_type=jnp.float32)
    dsf = (soft_f * (grad_f - jnp.sum(grad_f * soft_f, axis=-1, keepdims=True))).astype(
        jnp.bfloat16
    )
    dq_local = temper * jnp.einsum(
        "bhlm,bmhd->blhd", dsf, landk_four, preferred_element_type=jnp.float32
    )
    key_part = temper * jnp.einsum("bhlm,blhd->bmhd", dsf, quer, preferred_element_type=jnp.float32)
    grad_inv = jnp.einsum("bmhd,bnhd->bhmn", gcomb_four, mixed_four, precision=high)
    grad_mix = jnp.einsum("bhnm,bnhd->bmhd", inverse, gcomb_four, precision=high)
    grad_a = pull(grad_inv)[0]
    dsa = soft_a * (grad_a - jnp.sum(grad_a * soft_a, axis=-1, keepdims=True))
    query_land_a = temper * jnp.einsum(
        "bhmn,bnhd->bmhd", dsa, landk_four.astype(jnp.float32), precision=high
    )
    key_land_a = temper * jnp.einsum(
        "bhmn,bmhd->bnhd", dsa, landq_four.astype(jnp.float32), precision=high
    )
    gmix = grad_mix.astype(jnp.bfloat16)
    grad_b = jnp.einsum("bmhd,blhd->bhml", gmix, vals_four, preferred_element_type=jnp.float32)
    row_dot = jnp.einsum("bmhd,bmhd->bhm", gmix.astype(jnp.float32), mixed_four)
    dsb = (soft_b * (grad_b - row_dot[..., None])).astype(jnp.bfloat16)
    grad_vals = jnp.einsum("bhml,bmhd->blhd", weights_b, gmix, preferred_element_type=jnp.float32)
    query_part = temper * jnp.einsum(
        "bhml,blhd->bmhd", dsb, keys_four, preferred_element_type=jnp.float32
    )
    dk_local = temper * jnp.einsum(
        "bhml,bmhd->blhd", dsb, landq_four, preferred_element_type=jnp.float32
    )
    query_part = query_part.reshape(count, M, width)
    key_part = key_part.reshape(count, M, width)
    start = lax.axis_index("seq") * land_dev
    total_q, total_k = lax.psum((query_part, key_part), "seq")
    own_q = lax.dynamic_slice_in_dim(total_q, start, land_dev, 1)
    own_k = lax.dynamic_slice_in_dim(total_k, start, land_dev, 1)
    own_qa = lax.dynamic_slice_in_dim(query_land_a.reshape(count, M, width), start, land_dev, 1)
    own_ka = lax.dynamic_slice_in_dim(key_land_a.reshape(count, M, width), start, land_dev, 1)
    query_land = (own_q + own_qa) / seg_len
    key_land = (own_k + own_ka) / seg_len
    grad_q = dq_local.reshape(count, land_dev, seg_len, width) + query_land[:, :, None, :]
    grad_k = dk_local.reshape(count, land_dev, seg_len, width) + key_land[:, :, None, :]
    grad_queries = grad_q.reshape(count, rows, width).astype(jnp.bfloat16)
    grad_keys = grad_k.reshape(count, rows, width).astype(jnp.bfloat16)
    grad_values = grad_vals.reshape(count, rows, width).astype(jnp.bfloat16)
    return (grad_queries, grad_keys, grad_values)


def solution(mesh):
    return jax.shard_map(
        per_device,
        mesh=mesh,
        in_specs=(
            P(("groups", "batch"), "seq", "head"),
            P(("groups", "batch"), "seq", "head"),
            P(("groups", "batch"), "seq", "head"),
            P(("groups", "batch"), "seq", "head"),
        ),
        out_specs=(
            P(("groups", "batch"), "seq", "head"),
            P(("groups", "batch"), "seq", "head"),
            P(("groups", "batch"), "seq", "head"),
        ),
        check_vma=False,
    )
```

profile of v0, /device:TPU:0, one launch (start us, length us, event | category | flops | bytes accessed | tf_op | source)
XLA Modules:
  0.0 380.4 jit_solution(17328483483391836617)
XLA Ops:
  10.2 15.6 %all-gather.1 = bf16[256,512]{1,0:T(8,128)(2,1)S(1)} all-gather(bf16[64,512]{1,0:T(8,128)(2,1)S(1)} %multiply_convert_fusion.1), channel_id=3, replica_groups=mesh['groups'=2,'seq'=4,'head'=2,'batch'=2] {'seq'}, dimensions={0}, use_global_device_ids=true | all-gather | bytes 327680 | tf_op jit(solution)/shard_map/all_gather | solution.py:60
  26.0 14.6 %all-gather = bf16[256,512]{1,0:T(8,128)(2,1)S(1)} all-gather(bf16[64,512]{1,0:T(8,128)(2,1)S(1)} %multiply_convert_fusion.2), channel_id=2, replica_groups=mesh['groups'=2,'seq'=4,'head'=2,'batch'=2] {'seq'}, dimensions={0}, use_global_device_ids=true | all-gather | bytes 327680 | tf_op jit(solution)/shard_map/all_gather | solution.py:61
  46.7 13.1 %all-gather.2 = f32[32,256]{1,0:T(8,128)S(1)} all-gather(f32[8,256]{1,0:T(8,128)S(1)} %get-tuple-element.173), channel_id=4, replica_groups=mesh['groups'=2,'seq'=4,'head'=2,'batch'=2] {'seq'}, dimensions={0}, use_global_device_ids=true | all-gather | bytes 40960 | tf_op jit(solution)/shard_map/all_gather | solution.py:12
  61.7 13.1 %all-gather.3 = f32[32,256]{1,0:T(8,128)S(1)} all-gather(f32[8,256]{1,0:T(8,128)S(1)} %exponential_reduce_fusion), channel_id=5, replica_groups=mesh['groups'=2,'seq'=4,'head'=2,'batch'=2] {'seq'}, dimensions={0}, use_global_device_ids=true | all-gather | bytes 40960 | tf_op jit(solution)/shard_map/all_gather | solution.py:12
  74.9 5.0 %fusion.216 = (f32[8,1024]{1,0:T(8,128)S(1)}, f32[8,1024,256]{1,2,0:T(8,128)}) fusion(bf16[256,8,64]{0,2,1:T(8,128)(2,1)S(1)} %bitcast.289, bf16[1024,8,64]{0,2,1:T(8,128)(2,1)S(1)} %bitcast.287), kind=kOutput, calls=%fused_computation.218 | convolution fusion | flops 274727168 | bytes 9732096 | tf_op jit(solution)/shard_map/sub | solution.py:36
  79.9 6.2 %fusion.139 = f32[256,8,64]{0,2,1:T(8,128)} fusion(bf16[1024,8,64]{0,2,1:T(8,128)(2,1)S(1)} %bitcast.297, f32[8,256,1024]{2,1,0:T(8,128)} %copy-done.18, f32[8,256]{1,0:T(8,128)S(1)} %bitcast.303, f32[8,256]{1,0:T(8,128)S(1)} %bitcast.300), kind=kOutput, calls=%fused_computation.149 | convolution fusion | flops 276824064 | bytes 9977856 | tf_op jit(solution)/shard_map/bhml,blhd->bmhd/dot_general | solution.py:85
  96.2 8.1 %online-softmax = f32[8,256,256]{2,1,0:T(8,128)} custom-call(f32[8,256,256]{2,1,0:T(8,128)} %copy-done, f32[8,256,256]{2,1,0:T(8,128)} %copy.91), custom_call_target="tpu_custom_call" | custom-call | tf_op online-softmax
  104.3 4.6 %fusion.28 = f32[8,256,256]{2,1,0:T(8,128)S(1)} fusion(f32[8,256,256]{2,1,0:T(8,128)} %online-softmax, f32[256,256]{1,0:T(8,128)S(1)} %fusion.193), kind=kOutput, calls=%fused_computation.38 | convolution fusion | flops 1611137024 | bytes 4456448 | tf_op jit(solution)/shard_map/jvp()/dot_general | solution.py:29
  112.5 5.4 %fusion.116 = f32[8,256,256]{2,1,0:T(8,128)} fusion(f32[8,256,256]{2,1,0:T(8,128)S(1)} %fusion.108, f32[256,256]{1,0:T(8,128)S(1)} %fusion.195, f32[8]{0:T(128)S(1)} %get-tuple-element.168, f32[8,256,256]{2,1,0:T(8,128)S(1)} %copy-done.1, f32[8,256]{1,0:T(8,128)S(1)} %fusion.115, f32[8,256]{1,0:T(8,128)S(1)} %get-tuple-element.177), kind=kOutput, calls=%fused_computation.141 | convolution fusion | flops 1613234176 | bytes 6570016 | tf_op jit(solution)/shard_map/jvp()/dot_general | solution.py:31
  117.9 8.3 %online-softmax.1 = f32[8,256,256]{2,1,0:T(8,128)} custom-call(f32[8,256,256]{2,1,0:T(8,128)} %copy-done, f32[8,256,256]{2,1,0:T(8,128)} %fusion.116), custom_call_target="tpu_custom_call" | custom-call | tf_op online-softmax
  126.3 4.6 %fusion.24 = f32[8,256,256]{2,1,0:T(8,128)S(1)} fusion(f32[8,256,256]{2,1,0:T(8,128)} %online-softmax.1, f32[256,256]{1,0:T(8,128)S(1)} %fusion.193), kind=kOutput, calls=%fused_computation.34 | convolution fusion | flops 1611137024 | bytes 4456448 | tf_op jit(solution)/shard_map/jvp()/dot_general | solution.py:29
  134.5 3.6 fusion.122
  138.1 8.3 %online-softmax.2 = f32[8,256,256]{2,1,0:T(8,128)} custom-call(f32[8,256,256]{2,1,0:T(8,128)} %copy-done, f32[8,256,256]{2,1,0:T(8,128)} %fusion.122), custom_call_target="tpu_custom_call" | custom-call | tf_op online-softmax
  146.5 4.6 %fusion.20 = f32[8,256,256]{2,1,0:T(8,128)S(1)} fusion(f32[8,256,256]{2,1,0:T(8,128)} %online-softmax.2, f32[256,256]{1,0:T(8,128)S(1)} %fusion.193), kind=kOutput, calls=%fused_computation.30 | convolution fusion | flops 1611137024 | bytes 4456448 | tf_op jit(solution)/shard_map/jvp()/dot_general | solution.py:29
  154.7 3.6 fusion.125
  158.3 8.5 %online-softmax.3 = f32[8,256,256]{2,1,0:T(8,128)} custom-call(f32[8,256,256]{2,1,0:T(8,128)} %copy-done, f32[8,256,256]{2,1,0:T(8,128)} %fusion.125), custom_call_target="tpu_custom_call" | custom-call | tf_op online-softmax
  166.8 5.9 %fusion.16 = f32[8,256,256]{2,1,0:T(8,128)} fusion(f32[8,256,256]{2,1,0:T(8,128)} %online-softmax.3, f32[256,256]{1,0:T(8,128)S(1)} %fusion.193), kind=kOutput, calls=%fused_computation.26 | convolution fusion | flops 1611137024 | bytes 4456448 | tf_op jit(solution)/shard_map/jvp()/dot_general | solution.py:29
  172.9 4.0 %fusion.87 = f32[8,256,256]{2,1,0:T(8,128)S(1)} fusion(f32[8,256,256]{2,1,0:T(8,128)S(1)} %copy-done.9, f32[8,256,256]{2,1,0:T(8,128)} %fusion.16, f32[256,256]{1,0:T(8,128)S(1)} %fusion.194), kind=kOutput, calls=%fused_computation.114 | convolution fusion | flops 1611137024 | bytes 6553600 | tf_op jit(solution)/shard_map/jvp()/dot_general | solution.py:30
  178.2 3.5 fusion.84
  181.7 3.9 %fusion.157 = bf16[256,8,64]{0,2,1:T(8,128)(2,1)S(1)} fusion(f32[256,8,64]{0,2,1:T(8,128)} %get-tuple-element.161, f32[8,256,256]{2,1,0:T(8,128)} %fusion.84), kind=kOutput, calls=%fused_computation.157 | convolution fusion | flops 403308544 | bytes 2883584 | tf_op jit(solution)/shard_map/bhmn,bnhd->bmhd/dot_general | solution.py:96
  190.2 5.9 %fusion.136 = bf16[8,64,1024]{2,1,0:T(8,128)(2,1)} fusion(bf16[8,64,256]{2,1,0:T(8,128)(2,1)S(1)} %get-tuple-element.186, f32[8,256,1024]{2,1,0:T(8,128)} %copy-done.18, f32[8,256]{1,0:T(8,128)S(1)} %bitcast.304, f32[8,256]{1,0:T(8,128)S(1)} %bitcast.301), kind=kOutput, calls=%fused_computation.148 | convolution fusion | flops 277348352 | bytes 9715712 | tf_op jit(solution)/shard_map/bhml,bmhd->blhd/dot_general | solution.py:121
  204.0 3.5 fusion.77
  215.7 3.5 negate_add_fusion.3
  222.7 4.6 %fusion.208 = f32[8,256,256]{2,1,0:T(8,128)S(1)} fusion(f32[8,256,256]{2,1,0:T(8,128)S(1)} %negate_add_fusion.3, f32[8,256,256]{2,1,0:T(8,128)S(1)} %copy-done.2, f32[8,256]{1,0:T(8,128)S(1)} %fusion.115, f32[8,256]{1,0:T(8,128)S(1)} %get-tuple-element.177), kind=kOutput, calls=%fused_computation.216 | convolution fusion | flops 1611661312 | bytes 6307840 | tf_op jit(solution)/shard_map/transpose(jvp())/dot_general | solution.py:28
  237.7 3.7 fusion.64
  250.7 4.5 %add_multiply_fusion.1 = f32[8,256,256]{2,1,0:T(8,128)S(1)} fusion(f32[8,256,256]{2,1,0:T(8,128)S(1)} %fusion.89, f32[8,256,256]{2,1,0:T(8,128)S(1)} %negate_add_fusion.2, f32[8,256,256]{2,1,0:T(8,128)S(1)} %copy-done.2, f32[8,256]{1,0:T(8,128)S(1)} %fusion.115, f32[8,256]{1,0:T(8,128)S(1)} %get-tuple-element.177), kind=kOutput, calls=%fused_computation.65 | convolution fusion | flops 1612709888 | bytes 8404992 | tf_op jit(solution)/shard_map/transpose(jvp())/dot_general | solution.py:28
  276.2 4.3 %add_multiply_fusion = f32[8,256,256]{2,1,0:T(8,128)S(1)} fusion(f32[8,256,256]{2,1,0:T(8,128)S(1)} %fusion.96, f32[8,256,256]{2,1,0:T(8,128)S(1)} %negate_add_fusion.1, f32[8,256,256]{2,1,0:T(8,128)S(1)} %copy-done.2, f32[8,256]{1,0:T(8,128)S(1)} %fusion.115, f32[8,256]{1,0:T(8,128)S(1)} %get-tuple-element.177), kind=kOutput, calls=%fused_computation.63 | convolution fusion | flops 1612709888 | bytes 8404992 | tf_op jit(solution)/shard_map/transpose(jvp())/dot_general | solution.py:28
  295.0 5.5 %fusion.212 = f32[8,256,256]{1,2,0:T(8,128)} fusion(f32[8,256,256]{2,1,0:T(8,128)S(1)} %negate_add_fusion, f32[8,256,256]{2,1,0:T(8,128)S(1)} %copy-done.2, f32[8,256]{1,0:T(8,128)S(1)} %fusion.115, f32[8,256]{1,0:T(8,128)S(1)} %get-tuple-element.177), kind=kOutput, calls=%fused_computation.217 | convolution fusion | flops 1611661312 | bytes 6307840 | tf_op jit(solution)/shard_map/transpose(jvp())/dot_general | solution.py:28
  308.6 4.0 %fusion.41 = (f32[8]{0:T(128)S(1)}, f32[8,256,256]{1,2,0:T(8,128)}) fusion(f32[8]{0:T(128)S(1)} %get-tuple-element.167, f32[8,256]{1,0:T(8,128)S(1)} %fusion.115, f32[8,256,256]{2,1,0:T(8,128)S(1)} %copy-done.2, f32[8,256]{1,0:T(8,128)S(1)} %get-tuple-element.177, f32[8,256,256]{1,2,0:T(8,128)S(1)} %copy-done.53, f32[8,256,256]{2,1,0:T(8,128)S(1)} %add_multiply_fusion, ...), kind=kOutput, calls=%fused_computation.58 | convolution fusion | flops 1614282752 | bytes 10764352 | tf_op jit(solution)/shard_map/transpose(jvp())/dot_general | solution.py:31
  312.8 7.9 %fusion.42 = (f32[8,256]{1,0:T(8,128)S(1)}, f32[1,8,256,256]{3,2,1,0:T(8,128)}) fusion(f32[8,256]{1,0:T(8,128)S(1)} %fusion.115, f32[8,256,256]{2,1,0:T(8,128)S(1)} %copy-done.2, f32[8,256]{1,0:T(8,128)S(1)} %get-tuple-element.177, f32[8,256]{1,0:T(8,128)S(1)} %broadcast_select_fusion, f32[8,256]{1,0:T(8,128)S(1)} %broadcast_select_fusion.1, ...), kind=kOutput, calls=%fused_computation.61 | convolution fusion | flops 1622669312 | bytes 14721056 | tf_op jit(solution)/shard_map/transpose(jvp())/dot_general | solution.py:28
  331.0 4.0 %fusion.148 = f32[8,64,256]{2,1,0:T(8,128)} fusion(bf16[256,8,64]{0,2,1:T(8,128)(2,1)S(1)} %bitcast.284, f32[1,8,256,256]{3,2,1,0:T(8,128)} %get-tuple-element.184, f32[8,256]{1,0:T(8,128)S(1)} %get-tuple-element.183, f32[8,256,256]{2,1,0:T(8,128)S(1)} %copy-done.2, f32[8,256]{1,0:T(8,128)S(1)} %fusion.115, f32[8,256]{1,0:T(8,128)S(1)} %get-tuple-element.177), kind=kOutput, calls=%fused_computation.152 | convolution fusion | flops 404881408 | bytes 5005312 | tf_op jit(solution)/shard_map/bhmn,bmhd->bnhd/dot_general | solution.py:114
  337.4 28.7 %all-reduce.5.cloned.1.call-done = (f32[1,256,512]{1,2,0:T(8,128)}, f32[1,256,512]{1,2,0:T(8,128)}) async-done(((f32[1,256,512]{1,2,0:T(8,128)}, f32[1,256,512]{1,2,0:T(8,128)}), (f32[1,256,512]{1,2,0:T(8,128)}, f32[1,256,512]{1,2,0:T(8,128)})) %all-reduce.5.cloned.1.call-update) | async-done | bytes 1048592 | tf_op jit(solution)/shard_map/psum | solution.py:131
  (206 shorter events, 140.4 us)
Async XLA Ops:
  7.2 174.5 %all-reduce.7.cloned.1.call-start = ((), (), s32[]{:S(2)}) async-start(), calls=%async_computation.1 | async-start | bytes 2097152 | tf_op jit(solution)/shard_map/psum | solution.py:92
  8.9 36.5 %copy-start.33 = (bf16[1,1024,512]{1,2,0:T(8,128)(2,1)}, bf16[1,1024,512]{1,2,0:T(8,128)(2,1)S(1)}, u32[]{:S(2)}) copy-start(bf16[1,1024,512]{1,2,0:T(8,128)(2,1)S(1)} %copy.88) | copy-start | bytes 3145732
  9.8 65.1 %copy-start.41 = (bf16[1,1024,512]{1,2,0:T(8,128)(2,1)}, bf16[1,1024,512]{1,2,0:T(8,128)(2,1)S(1)}, u32[]{:S(2)}) copy-start(bf16[1,1024,512]{1,2,0:T(8,128)(2,1)S(1)} %copy.86) | copy-start | bytes 3145732
  40.7 48.3 %copy-start.43 = (bf16[256,512]{0,1:T(8,128)(2,1)}, bf16[256,512]{0,1:T(8,128)(2,1)S(1)}, u32[]{:S(2)}) copy-start(bf16[256,512]{0,1:T(8,128)(2,1)S(1)} %copy.85) | copy-start | bytes 786436
  46.7 14.9 %copy-start.18 = (f32[8,256,1024]{2,1,0:T(8,128)}, f32[8,256,1024]{2,1,0:T(8,128)S(1)}, u32[]{:S(2)}) copy-start(f32[8,256,1024]{2,1,0:T(8,128)S(1)} %get-tuple-element.174) | copy-start | bytes 25165828
  74.9 5.0 %copy-start.51 = (bf16[1,1024,512]{1,2,0:T(8,128)(2,1)S(1)}, bf16[1,1024,512]{1,2,0:T(8,128)(2,1)}, u32[]{:S(2)}) copy-start(bf16[1,1024,512]{1,2,0:T(8,128)(2,1)} %copy.89) | copy-start | bytes 3145732
  79.9 6.2 %copy-start.35 = (f32[8,1024,256]{1,2,0:T(8,128)S(1)}, f32[8,1024,256]{1,2,0:T(8,128)}, u32[]{:S(2)}) copy-start(f32[8,1024,256]{1,2,0:T(8,128)} %get-tuple-element.176) | copy-start | bytes 25165828
  79.9 6.2 %copy-start.49 = (bf16[1,1024,512]{1,2,0:T(8,128)(2,1)S(1)}, bf16[1,1024,512]{1,2,0:T(8,128)(2,1)}, u32[]{:S(2)}) copy-start(bf16[1,1024,512]{1,2,0:T(8,128)(2,1)} %copy.93) | copy-start | bytes 3145732
  88.4 277.7 %all-reduce.5.cloned.1.call-start = ((), (), s32[]{:S(2)}) async-start(), calls=%async_computation | async-start | bytes 2097152 | tf_op jit(solution)/shard_map/psum | solution.py:131
  104.3 4.6 %copy-start.3 = (f32[8,256,256]{2,1,0:T(8,128)S(1)}, f32[8,256,256]{2,1,0:T(8,128)}, u32[]{:S(2)}) copy-start(f32[8,256,256]{2,1,0:T(8,128)} %online-softmax) | copy-start | bytes 6291460
  108.9 3.6 copy-start.1
  126.3 4.6 %copy-start.5 = (f32[8,256,256]{2,1,0:T(8,128)S(1)}, f32[8,256,256]{2,1,0:T(8,128)}, u32[]{:S(2)}) copy-start(f32[8,256,256]{2,1,0:T(8,128)} %online-softmax.1) | copy-start | bytes 6291460
  130.9 3.6 copy-start.16
  146.5 4.6 %copy-start.7 = (f32[8,256,256]{2,1,0:T(8,128)S(1)}, f32[8,256,256]{2,1,0:T(8,128)}, u32[]{:S(2)}) copy-start(f32[8,256,256]{2,1,0:T(8,128)} %online-softmax.2) | copy-start | bytes 6291460
  151.1 3.7 copy-start.10
  166.8 6.1 %copy-start.9 = (f32[8,256,256]{2,1,0:T(8,128)S(1)}, f32[8,256,256]{2,1,0:T(8,128)}, u32[]{:S(2)}) copy-start(f32[8,256,256]{2,1,0:T(8,128)} %online-softmax.3) | copy-start | bytes 6291460
  172.9 5.3 %copy-start.12 = (f32[8,256,256]{2,1,0:T(8,128)S(1)}, f32[8,256,256]{2,1,0:T(8,128)}, u32[]{:S(2)}) copy-start(f32[8,256,256]{2,1,0:T(8,128)} %fusion.125) | copy-start | bytes 6291460
  181.7 3.9 %copy-start.32 = (f32[8,256,256]{2,1,0:T(8,128)S(1)}, f32[8,256,256]{2,1,0:T(8,128)}, u32[]{:S(2)}) copy-start(f32[8,256,256]{2,1,0:T(8,128)} %fusion.84) | copy-start | bytes 6291460
  181.7 3.9 %copy-start.38 = (f32[256,8,64]{0,2,1:T(8,128)S(1)}, f32[256,8,64]{0,2,1:T(8,128)}, u32[]{:S(2)}) copy-start(f32[256,8,64]{0,2,1:T(8,128)} %get-tuple-element.161) | copy-start | bytes 1572868
  188.3 7.8 %slice-start = ((s8[8388608]{0:T(1024)(128)(4,1)}), s8[4194304]{0:T(1024)(128)(4,1)S(1)}, s32[]{:S(2)}) async-start(s8[8388608]{0:T(1024)(128)(4,1)} %bitcast.271), calls=%async_computation.2 | async-start | bytes 8388608
  190.2 5.9 %slice-start.1 = ((s8[8388608]{0:T(1024)(128)(4,1)}), s8[4194304]{0:T(1024)(128)(4,1)S(1)}, s32[]{:S(2)}) async-start(s8[8388608]{0:T(1024)(128)(4,1)} %bitcast.271), calls=%async_computation.3 | async-start | bytes 8388608
  190.2 5.9 %copy-start.52 = (bf16[1,1024,512]{1,2,0:T(8,128)(2,1)S(1)}, bf16[1,1024,512]{1,2,0:T(8,128)(2,1)}, u32[]{:S(2)}) copy-start(bf16[1,1024,512]{1,2,0:T(8,128)(2,1)} %copy.89) | copy-start | bytes 3145732
  222.7 4.7 %copy-start.31 = (f32[8,256,256]{2,1,0:T(8,128)S(1)}, f32[8,256,256]{2,1,0:T(8,128)}, u32[]{:S(2)}) copy-start(f32[8,256,256]{2,1,0:T(8,128)} %copy-done.30) | copy-start | bytes 6291460
  250.7 4.5 %copy-start.24 = (f32[8,256,256]{2,1,0:T(8,128)S(1)}, f32[8,256,256]{2,1,0:T(8,128)}, u32[]{:S(2)}) copy-start(f32[8,256,256]{2,1,0:T(8,128)} %copy-done.23) | copy-start | bytes 6291460
  289.2 11.3 %slice-start.2 = ((s8[8388608]{0:T(1024)(128)(4,1)}), s8[4194304]{0:T(1024)(128)(4,1)S(1)}, s32[]{:S(2)}) async-start(s8[8388608]{0:T(1024)(128)(4,1)} %bitcast.277), calls=%async_computation.4 | async-start | bytes 8388608
  291.4 9.1 %slice-start.3 = ((s8[8388608]{0:T(1024)(128)(4,1)}), s8[4194304]{0:T(1024)(128)(4,1)S(1)}, s32[]{:S(2)}) async-start(s8[8388608]{0:T(1024)(128)(4,1)} %bitcast.277), calls=%async_computation.5 | async-start | bytes 8388608
  294.9 5.5 %copy-start.47 = (f32[8,256,256]{2,1,0:T(8,128)}, f32[8,256,256]{2,1,0:T(8,128)S(1)}, u32[]{:S(2)}) copy-start(f32[8,256,256]{2,1,0:T(8,128)S(1)} %negate_add_fusion) | copy-start | bytes 6291460
  294.9 5.5 %copy-start.50 = (bf16[1,1024,512]{1,2,0:T(8,128)(2,1)S(1)}, bf16[1,1024,512]{1,2,0:T(8,128)(2,1)}, u32[]{:S(2)}) copy-start(bf16[1,1024,512]{1,2,0:T(8,128)(2,1)} %copy.93) | copy-start | bytes 3145732
  304.7 3.9 %copy-start.53 = (f32[8,256,256]{1,2,0:T(8,128)S(1)}, f32[8,256,256]{1,2,0:T(8,128)}, u32[]{:S(2)}) copy-start(f32[8,256,256]{1,2,0:T(8,128)} %fusion.212) | copy-start | bytes 6291460
  312.8 8.0 %copy-start.15 = (bf16[8,1024,256]{1,2,0:T(8,128)(2,1)S(1)}, bf16[8,1024,256]{1,2,0:T(8,128)(2,1)}, u32[]{:S(2)}) copy-start(bf16[8,1024,256]{1,2,0:T(8,128)(2,1)} %copy-done.14) | copy-start | bytes 12582916
  312.8 8.0 %copy-start.44 = (bf16[256,512]{0,1:T(8,128)(2,1)S(1)}, bf16[256,512]{0,1:T(8,128)(2,1)}, u32[]{:S(2)}) copy-start(bf16[256,512]{0,1:T(8,128)(2,1)} %copy-done.43) | copy-start | bytes 786436
  331.0 4.0 %copy-start.54 = (f32[1,8,256,256]{3,2,1,0:T(8,128)S(1)}, f32[1,8,256,256]{3,2,1,0:T(8,128)}, u32[]{:S(2)}) copy-start(f32[1,8,256,256]{3,2,1,0:T(8,128)} %get-tuple-element.184) | copy-start | bytes 6291460
  (29 other events, 68.2 us)
Sparse Core Ops, SparseCore 0:
  88.5 53.1 all-reduce.6
  312.9 53.1 all-reduce.4
where the time goes:
time: 388 us; the launch traced here: 380 us
  matrix products  204 us (53%)
  blocking collectives  56.5 us (15%)
  Pallas kernels  33.2 us (9%)
  waiting for transfers between devices  28.8 us (7%)
  local copies, waits for them, and re-layouts  27.3 us (7%)
  between operations  15.4 us (4%)
  other arithmetic  14.3 us (4%)
    dot_general x12, matrix products, newton(): jnp.matmul(product, 7.0 * identity - product, precision=lax.Precision.HIG...  43.2 us
    dot_general x12, matrix products, newton(): jnp.matmul(approx, 13.0 * identity - inner, precision=lax.Precision.HIGHEST)  40.2 us
    dot_general x8, matrix products, newton(): product = jnp.matmul(matrix, approx, precision=lax.Precision.HIGHEST)  37.2 us
    dot_general x12, matrix products, newton(): jnp.matmul(product, 15.0 * identity - inner, precision=lax.Precision.HIGH...  33.9 us
    unnamed x4, Pallas kernels  33.2 us
    psum x1, waiting for transfers between devices, per_device(): total_q, total_k = lax.psum((query_part, key_part), 'seq')  28.7 us
    all_gather x2, blocking collectives, joined(): everything = jax.tree.map(lambda part: lax.all_gather(part, axis), x)  26.2 us
    unnamed x123, local copies, waits for them, and re-layouts  17.6 us
  transfers between devices with their start and end apart: 2, of which 1 were waited for; matrix products, arithmetic and copies ran while one was open for 21% of the time, Pallas kernels for 9%

commit v1 on v0

--- a/solution.py
+++ b/solution.py
@@ -6,6 +6,28 @@
 DH = 64
 M = 256
 ITERS = 4
+
+
+def in_order(parts, dim):
+    parts = jnp.moveaxis(parts, 0, dim)
+    shape = parts.shape
+    return parts.reshape(*shape[:dim], shape[dim] * shape[dim + 1], *shape[dim + 2 :])
+
+
+def gather_around(x, axis, dim):
+    devices = lax.axis_size(axis)
+    pairs = [(i, (i + 1) % devices) for i in range(devices)]
+    back = [(b, a) for a, b in pairs]
+    lower, upper = ([], [])
+    for step in range(devices - 1):
+        if step % 2 == 0:
+            lower.append(lax.ppermute(lower[-1] if lower else x, axis, pairs))
+        else:
+            upper.append(lax.ppermute(upper[-1] if upper else x, axis, back))
+    blocks = jnp.stack([*lower[::-1], x, *upper])
+    shift = lax.axis_index(axis) - len(lower)
+    blocks = blocks[(jnp.arange(devices) - shift) % devices]
+    return in_order(blocks, dim)
 
 
 def joined(x, axis, combine):
@@ -57,7 +79,7 @@
         return (summed / seg_len).astype(jnp.bfloat16)
 
     land_q, land_k = (
-        lax.all_gather(landmarks(query_rows), "seq", axis=1, tiled=True),
+        gather_around(landmarks(query_rows), "seq", 1),
         lax.all_gather(landmarks(key_rows), "seq", axis=1, tiled=True),
     )
     quer = query_rows.reshape(count, rows, heads, DH)

time: 388 us -> 423 us (1.090)
  waiting for transfers between devices: 28.8 us -> 73.3 us
  blocking collectives: 56.5 us -> 40.3 us
  starting transfers between devices: 0.54 us -> 8.23 us
    psum x1, waiting for transfers between devices: 0.01 us -> 41.9 us  [per_device(): mixed = lax.psum(mix_part, 'seq')]
    all_gather x1 -> x0, blocking collectives: 15.6 us -> none  [per_device(): lax.all_gather(landmarks(query_rows), 'seq', axis=1, tiled=True)]
    ppermute x0 -> x3, starting transfers between devices: none -> 7.69 us  [the longest x1 5.1 us: gather_around(): upper.append(lax.ppermute(upper[-1] if upper else x, axis, back))]
    ppermute x0 -> x3, waiting for transfers between devices: none -> 4.33 us  [the longest x2 4.33 us: gather_around(): lower.append(lax.ppermute(lower[-1] if lower else x, axis, pairs))]
    unnamed x123 -> x129, local copies, waits for them, and re-layouts: 17.6 us -> 17.2 us
  transfers between devices with their start and end apart: 2 -> 5, of which waited for: 1 -> 3; matrix products, arithmetic and copies ran while one was open for 21% -> 12% of each run, Pallas kernels for 9% -> 0%
where the time goes in v1:
time: 423 us; the launch traced here: 418 us
  matrix products  203 us (48%)
  waiting for transfers between devices  73.3 us (17%)
  blocking collectives  40.3 us (10%)
  Pallas kernels  32.9 us (8%)
  local copies, waits for them, and re-layouts  28 us (7%)
  other arithmetic  17.2 us (4%)
  between operations  15.5 us (4%)
  starting transfers between devices  8.23 us (2%)
    psum x1, waiting for transfers between devices, per_device(): mixed = lax.psum(mix_part, 'seq')  41.9 us
    dot_general x12, matrix products, newton(): jnp.matmul(approx, 13.0 * identity - inner, precision=lax.Precision.HIGHEST)  40.2 us
    dot_general x12, matrix products, newton(): jnp.matmul(product, 7.0 * identity - product, precision=lax.Precision.HIG...  39.5 us
    dot_general x8, matrix products, newton(): product = jnp.matmul(matrix, approx, precision=lax.Precision.HIGHEST)  37.2 us
    unnamed x4, Pallas kernels  32.9 us
    dot_general x12, matrix products, newton(): jnp.matmul(product, 15.0 * identity - inner, precision=lax.Precision.HIGH...  32.2 us
    psum x1, waiting for transfers between devices, per_device(): total_q, total_k = lax.psum((query_part, key_part), 'seq')  27.1 us
    all_gather x2, blocking collectives, joined(): everything = jax.tree.map(lambda part: lax.all_gather(part, axis), x)  26.2 us
  transfers between devices with their start and end apart: 5, of which 3 were waited for; matrix products, arithmetic and copies ran while one was open for 12% of the time, Pallas kernels for 0%

profile of v1, /device:TPU:0, one launch (start us, length us, event | category | flops | bytes accessed | tf_op | source)
XLA Modules:
  0.0 418.0 jit_solution(11604947085415753952)
XLA Ops:
  9.0 5.1 %collective-permute-start.2 = (bf16[1,64,512]{2,1,0:T(8,128)(2,1)S(1)}, bf16[1,64,512]{2,1,0:T(8,128)(2,1)}, u32[]{:S(2)}, u32[]{:S(2)}) collective-permute-start(bf16[1,64,512]{2,1,0:T(8,128)(2,1)S(1)} %get-tuple-element.172), channel_id=1, source_target_pairs={{4,0},{8,4},{12,8},{0,12},{5,1},{9,5},{13,9},{1,13},{6,2},{10,6},{... | collective-permute-start | bytes 196616 | tf_op jit(solution)/shard_map/ppermute | solution.py:26
  17.2 14.1 %all-gather = bf16[256,512]{1,0:T(8,128)(2,1)S(1)} all-gather(bf16[64,512]{1,0:T(8,128)(2,1)S(1)} %multiply_convert_fusion.2), channel_id=2, replica_groups=mesh['groups'=2,'seq'=4,'head'=2,'batch'=2] {'seq'}, dimensions={0}, use_global_device_ids=true | all-gather | bytes 327680 | tf_op jit(solution)/shard_map/all_gather | solution.py:83
  35.1 5.0 %fusion.220 = (f32[8,1024]{1,0:T(8,128)S(1)}, f32[8,1024,256]{1,2,0:T(8,128)}) fusion(bf16[256,8,64]{0,2,1:T(8,128)(2,1)S(1)} %bitcast.301, bf16[1024,8,64]{0,2,1:T(8,128)(2,1)S(1)} %bitcast.299), kind=kOutput, calls=%fused_computation.229 | convolution fusion | flops 274727168 | bytes 9732096 | tf_op jit(solution)/shard_map/sub | solution.py:58
  40.1 5.6 %fusion.142 = f32[256,8,64]{0,2,1:T(8,128)} fusion(bf16[1024,8,64]{0,2,1:T(8,128)(2,1)S(1)} %bitcast.307, f32[8,1024,256]{1,2,0:T(8,128)} %get-tuple-element.178, f32[8,1024]{1,0:T(8,128)S(1)} %get-tuple-element.177), kind=kOutput, calls=%fused_computation.151 | convolution fusion | flops 272629760 | bytes 9994240 | tf_op jit(solution)/shard_map/bhlm,blhd->bmhd/dot_general | solution.py:111
  48.3 4.3 %collective-permute-done.1 = bf16[1,64,512]{2,1,0:T(8,128)(2,1)S(1)} collective-permute-done((bf16[1,64,512]{2,1,0:T(8,128)(2,1)}, bf16[1,64,512]{2,1,0:T(8,128)(2,1)S(1)}, u32[]{:S(2)}, u32[]{:S(2)}) %collective-permute-start.1) | collective-permute-done | bytes 65568 | tf_op jit(solution)/shard_map/ppermute | solution.py:24
  62.5 8.1 %online-softmax = f32[8,256,256]{2,1,0:T(8,128)} custom-call(f32[8,256,256]{2,1,0:T(8,128)} %copy-done, f32[8,256,256]{2,1,0:T(8,128)} %copy.100), custom_call_target="tpu_custom_call" | custom-call | tf_op online-softmax
  70.6 4.6 %fusion.28 = f32[8,256,256]{2,1,0:T(8,128)S(1)} fusion(f32[8,256,256]{2,1,0:T(8,128)} %online-softmax, f32[256,256]{1,0:T(8,128)S(1)} %fusion.193), kind=kOutput, calls=%fused_computation.39 | convolution fusion | flops 1611137024 | bytes 4456448 | tf_op jit(solution)/shard_map/jvp()/dot_general | solution.py:51
  78.9 5.4 %fusion.116 = f32[8,256,256]{2,1,0:T(8,128)} fusion(f32[8,256,256]{2,1,0:T(8,128)S(1)} %fusion.108, f32[256,256]{1,0:T(8,128)S(1)} %fusion.195, f32[8]{0:T(128)S(1)} %get-tuple-element.168, f32[8,256,256]{2,1,0:T(8,128)S(1)} %copy-done.1, f32[8,256]{1,0:T(8,128)S(1)} %fusion.115, f32[8,256]{1,0:T(8,128)S(1)} %get-tuple-element.179), kind=kOutput, calls=%fused_computation.142 | convolution fusion | flops 1613234176 | bytes 6570016 | tf_op jit(solution)/shard_map/jvp()/dot_general | solution.py:53
  84.3 8.3 %online-softmax.1 = f32[8,256,256]{2,1,0:T(8,128)} custom-call(f32[8,256,256]{2,1,0:T(8,128)} %copy-done, f32[8,256,256]{2,1,0:T(8,128)} %fusion.116), custom_call_target="tpu_custom_call" | custom-call | tf_op online-softmax
  92.6 4.6 %fusion.24 = f32[8,256,256]{2,1,0:T(8,128)S(1)} fusion(f32[8,256,256]{2,1,0:T(8,128)} %online-softmax.1, f32[256,256]{1,0:T(8,128)S(1)} %fusion.193), kind=kOutput, calls=%fused_computation.35 | convolution fusion | flops 1611137024 | bytes 4456448 | tf_op jit(solution)/shard_map/jvp()/dot_general | solution.py:51
  100.8 3.6 fusion.122
  104.4 8.3 %online-softmax.2 = f32[8,256,256]{2,1,0:T(8,128)} custom-call(f32[8,256,256]{2,1,0:T(8,128)} %copy-done, f32[8,256,256]{2,1,0:T(8,128)} %fusion.122), custom_call_target="tpu_custom_call" | custom-call | tf_op online-softmax
  112.7 4.6 %fusion.20 = f32[8,256,256]{2,1,0:T(8,128)S(1)} fusion(f32[8,256,256]{2,1,0:T(8,128)} %online-softmax.2, f32[256,256]{1,0:T(8,128)S(1)} %fusion.193), kind=kOutput, calls=%fused_computation.31 | convolution fusion | flops 1611137024 | bytes 4456448 | tf_op jit(solution)/shard_map/jvp()/dot_general | solution.py:51
  121.0 3.6 fusion.125
  124.6 8.2 %online-softmax.3 = f32[8,256,256]{2,1,0:T(8,128)} custom-call(f32[8,256,256]{2,1,0:T(8,128)} %copy-done, f32[8,256,256]{2,1,0:T(8,128)} %fusion.125), custom_call_target="tpu_custom_call" | custom-call | tf_op online-softmax
  134.2 13.1 %all-gather.1 = f32[32,256]{1,0:T(8,128)S(1)} all-gather(f32[8,256]{1,0:T(8,128)S(1)} %get-tuple-element.175), channel_id=3, replica_groups=mesh['groups'=2,'seq'=4,'head'=2,'batch'=2] {'seq'}, dimensions={0}, use_global_device_ids=true | all-gather | bytes 40960 | tf_op jit(solution)/shard_map/all_gather | solution.py:34
  149.1 13.1 %all-gather.2 = f32[32,256]{1,0:T(8,128)S(1)} all-gather(f32[8,256]{1,0:T(8,128)S(1)} %exponential_reduce_fusion), channel_id=4, replica_groups=mesh['groups'=2,'seq'=4,'head'=2,'batch'=2] {'seq'}, dimensions={0}, use_global_device_ids=true | all-gather | bytes 40960 | tf_op jit(solution)/shard_map/all_gather | solution.py:34
  162.4 6.5 %fusion.139 = f32[256,8,64]{0,2,1:T(8,128)} fusion(bf16[1024,8,64]{0,2,1:T(8,128)(2,1)} %bitcast.309, f32[8,256,1024]{2,1,0:T(8,128)} %copy-done.18, f32[8,256]{1,0:T(8,128)S(1)} %bitcast.315, f32[8,256]{1,0:T(8,128)S(1)} %bitcast.312), kind=kOutput, calls=%fused_computation.150 | convolution fusion | flops 276824064 | bytes 9977856 | tf_op jit(solution)/shard_map/bhml,blhd->bmhd/dot_general | solution.py:107
  175.5 3.6 fusion.84
  179.0 41.9 %all-reduce.7.cloned.1.call-done = (f32[256,8,64]{0,2,1:T(8,128)}, f32[256,8,64]{0,2,1:T(8,128)}) async-done(((f32[256,8,64]{0,2,1:T(8,128)}, f32[256,8,64]{0,2,1:T(8,128)}), (f32[256,8,64]{0,2,1:T(8,128)}, f32[256,8,64]{0,2,1:T(8,128)})) %all-reduce.7.cloned.1.call-update) | async-done | bytes 1048592 | tf_op jit(solution)/shard_map/psum | solution.py:114
  220.9 3.9 fusion.157
  229.4 5.9 %fusion.136 = bf16[8,64,1024]{2,1,0:T(8,128)(2,1)} fusion(bf16[8,64,256]{2,1,0:T(8,128)(2,1)S(1)} %get-tuple-element.188, f32[8,256,1024]{2,1,0:T(8,128)} %copy-done.18, f32[8,256]{1,0:T(8,128)S(1)} %bitcast.316, f32[8,256]{1,0:T(8,128)S(1)} %bitcast.313), kind=kOutput, calls=%fused_computation.149 | convolution fusion | flops 277348352 | bytes 9715712 | tf_op jit(solution)/shard_map/bhml,bmhd->blhd/dot_general | solution.py:143
  243.1 3.5 fusion.77
  261.9 4.6 %fusion.212 = f32[8,256,256]{2,1,0:T(8,128)S(1)} fusion(f32[8,256,256]{2,1,0:T(8,128)S(1)} %negate_add_fusion.3, f32[8,256,256]{2,1,0:T(8,128)S(1)} %copy-done.2, f32[8,256]{1,0:T(8,128)S(1)} %fusion.115, f32[8,256]{1,0:T(8,128)S(1)} %get-tuple-element.179), kind=kOutput, calls=%fused_computation.227 | convolution fusion | flops 1611661312 | bytes 6307840 | tf_op jit(solution)/shard_map/transpose(jvp())/dot_general | solution.py:50
  276.9 3.7 fusion.64
  289.8 4.5 %add_multiply_fusion.1 = f32[8,256,256]{2,1,0:T(8,128)S(1)} fusion(f32[8,256,256]{2,1,0:T(8,128)S(1)} %fusion.89, f32[8,256,256]{2,1,0:T(8,128)S(1)} %negate_add_fusion.2, f32[8,256,256]{2,1,0:T(8,128)S(1)} %copy-done.2, f32[8,256]{1,0:T(8,128)S(1)} %fusion.115, f32[8,256]{1,0:T(8,128)S(1)} %get-tuple-element.179), kind=kOutput, calls=%fused_computation.66 | convolution fusion | flops 1612709888 | bytes 8404992 | tf_op jit(solution)/shard_map/transpose(jvp())/dot_general | solution.py:50
  315.3 4.3 %add_multiply_fusion = f32[8,256,256]{2,1,0:T(8,128)S(1)} fusion(f32[8,256,256]{2,1,0:T(8,128)S(1)} %fusion.96, f32[8,256,256]{2,1,0:T(8,128)S(1)} %negate_add_fusion.1, f32[8,256,256]{2,1,0:T(8,128)S(1)} %copy-done.2, f32[8,256]{1,0:T(8,128)S(1)} %fusion.115, f32[8,256]{1,0:T(8,128)S(1)} %get-tuple-element.179), kind=kOutput, calls=%fused_computation.64 | convolution fusion | flops 1612709888 | bytes 8404992 | tf_op jit(solution)/shard_map/transpose(jvp())/dot_general | solution.py:50
  334.1 5.5 %fusion.216 = f32[8,256,256]{1,2,0:T(8,128)} fusion(f32[8,256,256]{2,1,0:T(8,128)S(1)} %negate_add_fusion, f32[8,256,256]{2,1,0:T(8,128)S(1)} %copy-done.2, f32[8,256]{1,0:T(8,128)S(1)} %fusion.115, f32[8,256]{1,0:T(8,128)S(1)} %get-tuple-element.179), kind=kOutput, calls=%fused_computation.228 | convolution fusion | flops 1611661312 | bytes 6307840 | tf_op jit(solution)/shard_map/transpose(jvp())/dot_general | solution.py:50
  347.7 4.0 fusion.41
  351.9 7.9 %fusion.42 = (f32[8,256]{1,0:T(8,128)S(1)}, f32[1,8,256,256]{3,2,1,0:T(8,128)}) fusion(f32[8,256]{1,0:T(8,128)S(1)} %fusion.115, f32[8,256,256]{2,1,0:T(8,128)S(1)} %copy-done.2, f32[8,256]{1,0:T(8,128)S(1)} %get-tuple-element.179, f32[8,256]{1,0:T(8,128)S(1)} %broadcast_select_fusion, f32[8,256]{1,0:T(8,128)S(1)} %broadcast_select_fusion.1, ...), kind=kOutput, calls=%fused_computation.62 | convolution fusion | flops 1622669312 | bytes 14721056 | tf_op jit(solution)/shard_map/transpose(jvp())/dot_general | solution.py:50
  370.2 4.0 fusion.148
  376.6 27.1 %all-reduce.5.cloned.1.call-done = (f32[1,256,512]{1,2,0:T(8,128)}, f32[1,256,512]{1,2,0:T(8,128)}) async-done(((f32[1,256,512]{1,2,0:T(8,128)}, f32[1,256,512]{1,2,0:T(8,128)}), (f32[1,256,512]{1,2,0:T(8,128)}, f32[1,256,512]{1,2,0:T(8,128)})) %all-reduce.5.cloned.1.call-update) | async-done | bytes 1048592 | tf_op jit(solution)/shard_map/psum | solution.py:153
  (222 shorter events, 152.3 us)
Async XLA Ops:
  7.2 7.0 %copy-start.39 = (bf16[1,1024,512]{2,1,0:T(8,128)(2,1)S(1)}, bf16[1,1024,512]{2,1,0:T(8,128)(2,1)}, u32[]{:S(2)}) copy-start(bf16[1,1024,512]{2,1,0:T(8,128)(2,1)} %param.6) | copy-start | bytes 3145732
  7.2 213.7 %all-reduce.7.cloned.1.call-start = ((), (), s32[]{:S(2)}) async-start(), calls=%async_computation.1 | async-start | bytes 2097152 | tf_op jit(solution)/shard_map/psum | solution.py:114
  7.2 8.3 %copy-start.40 = (bf16[1,1024,512]{2,1,0:T(8,128)(2,1)S(1)}, bf16[1,1024,512]{2,1,0:T(8,128)(2,1)}, u32[]{:S(2)}) copy-start(bf16[1,1024,512]{2,1,0:T(8,128)(2,1)} %param.7) | copy-start | bytes 3145732
  9.0 39.3 %collective-permute-start.2 = (bf16[1,64,512]{2,1,0:T(8,128)(2,1)S(1)}, bf16[1,64,512]{2,1,0:T(8,128)(2,1)}, u32[]{:S(2)}, u32[]{:S(2)}) collective-permute-start(bf16[1,64,512]{2,1,0:T(8,128)(2,1)S(1)} %get-tuple-element.172), channel_id=1, source_target_pairs={{4,0},{8,4},{12,8},{0,12},{5,1},{9,5},{13,9},{1,13},{6,2},{10,6},{... | collective-permute-start | bytes 196616 | tf_op jit(solution)/shard_map/ppermute | solution.py:26
  14.1 31.6 %collective-permute-start = (bf16[1,64,512]{2,1,0:T(8,128)(2,1)S(1)}, bf16[1,64,512]{2,1,0:T(8,128)(2,1)}, u32[]{:S(2)}, u32[]{:S(2)}) collective-permute-start(bf16[1,64,512]{2,1,0:T(8,128)(2,1)S(1)} %get-tuple-element.172), channel_id=1, source_target_pairs={{0,4},{4,8},{8,12},{12,0},{1,5},{5,9},{9,13},{13,1},{2,6},{6,10},{... | collective-permute-start | bytes 196616 | tf_op jit(solution)/shard_map/ppermute | solution.py:24
  17.1 16.6 %copy-start.49 = (bf16[1,1024,512]{2,1,0:T(8,128)(2,1)S(1)}, bf16[1,1024,512]{2,1,0:T(8,128)(2,1)}, u32[]{:S(2)}) copy-start(bf16[1,1024,512]{2,1,0:T(8,128)(2,1)} %param.9) | copy-start | bytes 3145732
  31.4 23.3 %copy-start.43 = (bf16[256,512]{0,1:T(8,128)(2,1)}, bf16[256,512]{0,1:T(8,128)(2,1)S(1)}, u32[]{:S(2)}) copy-start(bf16[256,512]{0,1:T(8,128)(2,1)S(1)} %copy.90) | copy-start | bytes 786436
  35.1 5.0 %copy-start.50 = (bf16[1,1024,512]{1,2,0:T(8,128)(2,1)S(1)}, bf16[1,1024,512]{1,2,0:T(8,128)(2,1)}, u32[]{:S(2)}) copy-start(bf16[1,1024,512]{1,2,0:T(8,128)(2,1)} %copy.102) | copy-start | bytes 3145732
  40.1 5.6 %copy-start.53 = (f32[8,1024]{1,0:T(8,128)}, f32[8,1024]{1,0:T(8,128)S(1)}, u32[]{:S(2)}) copy-start(f32[8,1024]{1,0:T(8,128)S(1)} %get-tuple-element.177) | copy-start | bytes 98308
  45.7 6.9 %collective-permute-start.1 = (bf16[1,64,512]{2,1,0:T(8,128)(2,1)}, bf16[1,64,512]{2,1,0:T(8,128)(2,1)S(1)}, u32[]{:S(2)}, u32[]{:S(2)}) collective-permute-start(bf16[1,64,512]{2,1,0:T(8,128)(2,1)} %collective-permute-done), channel_id=1, source_target_pairs={{0,4},{4,8},{8,12},{12,0},{1,5},{5,9},{9,13},{13,1},{2,6},{6,10},{... | collective-permute-start | bytes 196616 | tf_op jit(solution)/shard_map/ppermute | solution.py:24
  70.6 4.6 %copy-start.3 = (f32[8,256,256]{2,1,0:T(8,128)S(1)}, f32[8,256,256]{2,1,0:T(8,128)}, u32[]{:S(2)}) copy-start(f32[8,256,256]{2,1,0:T(8,128)} %online-softmax) | copy-start | bytes 6291460
  92.6 4.6 %copy-start.5 = (f32[8,256,256]{2,1,0:T(8,128)S(1)}, f32[8,256,256]{2,1,0:T(8,128)}, u32[]{:S(2)}) copy-start(f32[8,256,256]{2,1,0:T(8,128)} %online-softmax.1) | copy-start | bytes 6291460
  112.7 4.6 %copy-start.7 = (f32[8,256,256]{2,1,0:T(8,128)S(1)}, f32[8,256,256]{2,1,0:T(8,128)}, u32[]{:S(2)}) copy-start(f32[8,256,256]{2,1,0:T(8,128)} %online-softmax.2) | copy-start | bytes 6291460
  124.6 8.2 %copy-start.34 = (bf16[1,1024,512]{1,2,0:T(8,128)(2,1)S(1)}, bf16[1,1024,512]{1,2,0:T(8,128)(2,1)}, u32[]{:S(2)}) copy-start(bf16[1,1024,512]{1,2,0:T(8,128)(2,1)} %copy.95) | copy-start | bytes 3145732
  134.2 14.9 %copy-start.18 = (f32[8,256,1024]{2,1,0:T(8,128)}, f32[8,256,1024]{2,1,0:T(8,128)S(1)}, u32[]{:S(2)}) copy-start(f32[8,256,1024]{2,1,0:T(8,128)S(1)} %get-tuple-element.176) | copy-start | bytes 25165828
  162.4 7.0 %copy-start.9 = (f32[8,256,256]{2,1,0:T(8,128)S(1)}, f32[8,256,256]{2,1,0:T(8,128)}, u32[]{:S(2)}) copy-start(f32[8,256,256]{2,1,0:T(8,128)} %online-softmax.3) | copy-start | bytes 6291460
  168.9 234.8 %all-reduce.5.cloned.1.call-start = ((), (), s32[]{:S(2)}) async-start(), calls=%async_computation | async-start | bytes 2097152 | tf_op jit(solution)/shard_map/psum | solution.py:153
  220.9 3.9 copy-start.33
  220.9 3.9 copy-start.38
  227.5 7.8 %slice-start = ((s8[8388608]{0:T(1024)(128)(4,1)}), s8[4194304]{0:T(1024)(128)(4,1)S(1)}, s32[]{:S(2)}) async-start(s8[8388608]{0:T(1024)(128)(4,1)} %bitcast.287), calls=%async_computation.2 | async-start | bytes 8388608
  229.4 5.9 %slice-start.1 = ((s8[8388608]{0:T(1024)(128)(4,1)}), s8[4194304]{0:T(1024)(128)(4,1)S(1)}, s32[]{:S(2)}) async-start(s8[8388608]{0:T(1024)(128)(4,1)} %bitcast.287), calls=%async_computation.3 | async-start | bytes 8388608
  229.4 5.9 %copy-start.52 = (bf16[1,1024,512]{1,2,0:T(8,128)(2,1)S(1)}, bf16[1,1024,512]{1,2,0:T(8,128)(2,1)}, u32[]{:S(2)}) copy-start(bf16[1,1024,512]{1,2,0:T(8,128)(2,1)} %copy.97) | copy-start | bytes 3145732
  261.9 4.7 %copy-start.32 = (f32[8,256,256]{2,1,0:T(8,128)S(1)}, f32[8,256,256]{2,1,0:T(8,128)}, u32[]{:S(2)}) copy-start(f32[8,256,256]{2,1,0:T(8,128)} %copy-done.31) | copy-start | bytes 6291460
  289.8 4.5 %copy-start.24 = (f32[8,256,256]{2,1,0:T(8,128)S(1)}, f32[8,256,256]{2,1,0:T(8,128)}, u32[]{:S(2)}) copy-start(f32[8,256,256]{2,1,0:T(8,128)} %copy-done.23) | copy-start | bytes 6291460
  328.3 11.3 %slice-start.2 = ((s8[8388608]{0:T(1024)(128)(4,1)}), s8[4194304]{0:T(1024)(128)(4,1)S(1)}, s32[]{:S(2)}) async-start(s8[8388608]{0:T(1024)(128)(4,1)} %bitcast.293), calls=%async_computation.4 | async-start | bytes 8388608
  330.5 9.1 %slice-start.3 = ((s8[8388608]{0:T(1024)(128)(4,1)}), s8[4194304]{0:T(1024)(128)(4,1)S(1)}, s32[]{:S(2)}) async-start(s8[8388608]{0:T(1024)(128)(4,1)} %bitcast.293), calls=%async_computation.5 | async-start | bytes 8388608
  334.1 5.5 %copy-start.47 = (f32[8,256,256]{2,1,0:T(8,128)}, f32[8,256,256]{2,1,0:T(8,128)S(1)}, u32[]{:S(2)}) copy-start(f32[8,256,256]{2,1,0:T(8,128)S(1)} %negate_add_fusion) | copy-start | bytes 6291460
  334.1 5.5 %copy-start.51 = (bf16[1,1024,512]{1,2,0:T(8,128)(2,1)S(1)}, bf16[1,1024,512]{1,2,0:T(8,128)(2,1)}, u32[]{:S(2)}) copy-start(bf16[1,1024,512]{1,2,0:T(8,128)(2,1)} %copy.102) | copy-start | bytes 3145732
  334.1 5.5 %copy-start.54 = (f32[8,1024]{1,0:T(8,128)S(1)}, f32[8,1024]{1,0:T(8,128)}, u32[]{:S(2)}) copy-start(f32[8,1024]{1,0:T(8,128)} %copy-done.53) | copy-start | bytes 98308
  351.9 8.0 %copy-start.15 = (bf16[8,1024,256]{1,2,0:T(8,128)(2,1)S(1)}, bf16[8,1024,256]{1,2,0:T(8,128)(2,1)}, u32[]{:S(2)}) copy-start(bf16[8,1024,256]{1,2,0:T(8,128)(2,1)} %copy-done.14) | copy-start | bytes 12582916
  351.9 8.0 %copy-start.44 = (bf16[256,512]{0,1:T(8,128)(2,1)S(1)}, bf16[256,512]{0,1:T(8,128)(2,1)}, u32[]{:S(2)}) copy-start(bf16[256,512]{0,1:T(8,128)(2,1)} %copy-done.43) | copy-start | bytes 786436
  370.2 4.0 copy-start.57
  (35 other events, 92.7 us)
Sparse Core Ops, SparseCore 0:
  169.0 51.8 all-reduce.6
  352.0 51.5 all-reduce.4
